TPU v7x, 512 devices: a whole 4x8x8 slice. The times are simulated.
512 devices in a mesh: ctx: 128 (over z_hi, y, x), head: 4 (over z_lo, core).
Axes of the slice: x: 4, y: 8, z: 8 (z_hi: 4, z_lo: 2; z = z_hi * 2 + z_lo), core: 2. Of those that a mesh axis runs over, the one named last changes fastest.
Arguments:
- queries: bfloat16 [65536, 4096], P(('ctx', 'head')), may hold values from -8 to 8
- keys: bfloat16 [65536, 512], P(('ctx', 'head')), may hold values from -8 to 8
- values: bfloat16 [65536, 512], P(('ctx', 'head')), may hold values from -6 to 6
- doc_lengths: int32 [256], replicated, may hold values from 1 to 2048, 65536 in all
Outputs:
- attended: bfloat16 [65536, 4096], P('ctx', 'head')
Inputs may be any that keep to these rules, and one draw needn't show every extreme that they name: `doc_lengths`: the lengths sum to 65536 and the largest is exactly 2048.
All inputs are finite; a program needn't handle non-finite values.
Results may differ from a plain program's by a relative error of at most 0.012.
Values may be sent and summed in bfloat16 or wider, within the bound.
A program may use at most 64 MiB of HBM per device.

v0:
```python
import math

import jax
import jax.numpy as jnp
from jax import lax
from jax.sharding import PartitionSpec as P

QUERY_HEADS = 32
KEY_VALUE_HEADS = 4
HEAD_SIZE = 128
SPAN = 4


lowest_score = -1e30


def shifted(block, axis, distance):
    devices = range(lax.axis_size(axis))
    route = [(i - distance, i) for i in devices if i - distance in devices]
    return lax.ppermute(block, axis, route)


def segment_of(positions, doc_ends):
    return jnp.sum((positions[:, None] >= doc_ends[None, :]).astype(jnp.int32), axis=1)


def live_blocks(group_index, doc_lengths, doc_ends, block_rows):
    backward = jnp.arange(SPAN + 1, dtype=jnp.int32)
    first_start = jnp.sum(jnp.where(doc_ends <= group_index * block_rows, doc_lengths, 0))
    earlier = group_index - backward
    return (backward == 0) | (earlier >= 0) & (first_start < (earlier + 1) * block_rows)


def block_masks(group_index, doc_ends, block_rows):
    offsets = jnp.arange(block_rows, dtype=jnp.int32)
    backward = jnp.arange(SPAN + 1, dtype=jnp.int32)
    query_pos = group_index * block_rows + offsets
    query_seg = segment_of(query_pos, doc_ends)
    key_pos = (group_index - backward)[:, None] * block_rows + offsets[None, :]
    key_seg = segment_of(key_pos.reshape(-1), doc_ends).reshape(SPAN + 1, block_rows)
    same_doc = key_seg[:, None, :] == query_seg[None, :, None]
    causal = key_pos[:, None, :] <= query_pos[None, :, None]
    inside = key_pos[:, None, :] >= 0
    return same_doc & causal & inside


def attend(query_rows, stacked, allowed_all, live_mask):
    block_rows = query_rows.shape[0]
    head_count = query_rows.shape[1]
    head_width = query_rows.shape[2]
    shared_heads = QUERY_HEADS // KEY_VALUE_HEADS
    group_size = max(min(shared_heads // 2, head_count), 1)
    group_count = head_count // group_size
    score_scale = 1.0 / math.sqrt(head_width)
    grouped = jnp.transpose(query_rows, (1, 0, 2)).reshape(
        group_count, group_size, block_rows, head_width
    )

    def one_group(group_number):
        query_group = lax.dynamic_index_in_dim(grouped, group_number, 0, keepdims=False)
        kv_head = group_number * group_size // shared_heads
        kv_rows = lax.dynamic_index_in_dim(stacked, kv_head, 3, keepdims=False)
        current = (
            jnp.zeros((group_size, block_rows, head_width), jnp.float32),
            jnp.full((group_size, block_rows), lowest_score, jnp.float32),
            jnp.zeros((group_size, block_rows), jnp.float32),
        )
        for block_index in range(SPAN + 1):
            key_block = kv_rows[block_index, 0]
            value_block = kv_rows[block_index, 1]
            allowed = allowed_all[block_index][None, :, :]

            def update(state, key_block=key_block, value_block=value_block, allowed=allowed):
                accumulated, running, totals = state
                scores = (
                    jnp.einsum(
                        "gqd,kd->gqk", query_group, key_block, preferred_element_type=jnp.float32
                    )
                    * score_scale
                )
                scores = jnp.where(allowed, scores, lowest_score)
                highest = jnp.maximum(running, jnp.max(scores, axis=2))
                weights = jnp.where(allowed, jnp.exp(scores - highest[..., None]), 0.0)
                factor = jnp.exp(running - highest)
                totals = totals * factor + jnp.sum(weights, axis=2)
                product = jnp.einsum(
                    "gqk,kd->gqd",
                    weights.astype(jnp.bfloat16),
                    value_block,
                    preferred_element_type=jnp.float32,
                )
                accumulated = accumulated * factor[..., None] + product
                return (accumulated, highest, totals)

            current = lax.cond(live_mask[block_index], update, lambda state: state, current)
        return current

    summed, running, totals = lax.map(one_group, jnp.arange(group_count, dtype=jnp.int32))
    return (
        summed.reshape(head_count, block_rows, head_width),
        running.reshape(head_count, block_rows),
        totals.reshape(head_count, block_rows),
    )


def shards(queries, keys, values, doc_lengths):
    resident_rows = queries.shape[0]
    query_rows, key_rows, value_rows = (
        lax.all_to_all(
            queries.reshape(resident_rows, QUERY_HEADS, HEAD_SIZE),
            "head",
            split_axis=1,
            concat_axis=0,
            tiled=True,
        ),
        lax.all_to_all(
            keys.reshape(resident_rows, KEY_VALUE_HEADS, HEAD_SIZE),
            "head",
            split_axis=1,
            concat_axis=0,
            tiled=True,
        ),
        lax.all_to_all(
            values.reshape(resident_rows, KEY_VALUE_HEADS, HEAD_SIZE),
            "head",
            split_axis=1,
            concat_axis=0,
            tiled=True,
        ),
    )
    block_rows = query_rows.shape[0]
    own_pair = jnp.stack([key_rows, value_rows])
    blocks_list = [own_pair]
    previous = own_pair
    for distance in range(SPAN):
        previous = shifted(previous, "ctx", 1)
        blocks_list.append(previous)
    stacked = jnp.stack(blocks_list)
    group_index = lax.axis_index("ctx")
    doc_ends = jnp.cumsum(doc_lengths)
    allowed_all = block_masks(group_index, doc_ends, block_rows)
    live_mask = live_blocks(group_index, doc_lengths, doc_ends, block_rows)
    accumulated, unused_max, totals = attend(query_rows, stacked, allowed_all, live_mask)
    divided = accumulated / totals[..., None]
    return jnp.transpose(divided, (1, 0, 2)).reshape(block_rows, -1).astype(jnp.bfloat16)


def solution(mesh):
    placed = (P(("ctx", "head"), None), P(("ctx", "head"), None), P(("ctx", "head"), None), P())
    return jax.shard_map(
        shards, mesh=mesh, in_specs=placed, out_specs=P("ctx", "head"), check_vma=False
    )
```

profile of v0, /device:TPU:190, one launch (start us, length us, event | category | flops | bytes accessed | tf_op | source)
XLA Modules:
  0.0 192.2 jit_solution(16507462198542952130)
XLA Ops:
  1.6 3.6 %all-to-all-start.1 = ((bf16[128,4,128]{2,0,1:T(8,128)(2,1)}), bf16[128,4,128]{2,0,1:T(8,128)(2,1)S(1)}, u32[]{:S(2)}, u32[]{:S(2)}) async-start(bf16[128,4,128]{2,0,1:T(8,128)(2,1)} %copy_bitcast_fusion.3), calls=%async_computation.1 | async-start | bytes 262144 | tf_op jit(solution)/shard_map/all_to_all | solution.py:116
  9.9 3.3 %all-to-all-start.2 = ((bf16[128,4,128]{2,0,1:T(8,128)(2,1)}), bf16[128,4,128]{2,0,1:T(8,128)(2,1)S(1)}, u32[]{:S(2)}, u32[]{:S(2)}) async-start(bf16[128,4,128]{2,0,1:T(8,128)(2,1)} %copy_bitcast_fusion.2), calls=%async_computation.2 | async-start | bytes 262144 | tf_op jit(solution)/shard_map/all_to_all | solution.py:123
  17.8 3.5 %all-to-all-start = ((bf16[128,32,128]{2,0,1:T(8,128)(2,1)}), bf16[128,32,128]{2,0,1:T(8,128)(2,1)S(1)}, u32[]{:S(2)}, u32[]{:S(2)}) async-start(bf16[128,32,128]{2,0,1:T(8,128)(2,1)} %copy.86), calls=%async_computation | async-start | bytes 2097152 | tf_op jit(solution)/shard_map/all_to_all | solution.py:109
  21.4 6.1 %collective-permute-start = (bf16[2,512,1,128]{3,1,0,2:T(8,128)(2,1)S(1)}, bf16[2,512,1,128]{3,1,0,2:T(8,128)(2,1)S(1)}, u32[]{:S(2)}, u32[]{:S(2)}) collective-permute-start(bf16[2,512,1,128]{3,1,0,2:T(8,128)(2,1)S(1)} %pad_maximum_fusion), channel_id=1, source_target_pairs={{0,4},{4,8},{8,12},{12,16},{16,20},{20,24},{24,28},{28,32},{32,36}... | collective-permute-start | bytes 786440 | tf_op jit(solution)/shard_map/ppermute | solution.py:20
  27.8 8.9 %collective-permute-done = bf16[2,512,1,128]{3,1,0,2:T(8,128)(2,1)S(1)} collective-permute-done((bf16[2,512,1,128]{3,1,0,2:T(8,128)(2,1)S(1)}, bf16[2,512,1,128]{3,1,0,2:T(8,128)(2,1)S(1)}, u32[]{:S(2)}, u32[]{:S(2)}) %collective-permute-start) | collective-permute-done | bytes 262176 | tf_op jit(solution)/shard_map/ppermute | solution.py:20
  36.7 13.4 %collective-permute-start.1 = (bf16[2,512,1,128]{3,1,0,2:T(8,128)(2,1)S(1)}, bf16[2,512,1,128]{3,1,0,2:T(8,128)(2,1)S(1)}, u32[]{:S(2)}, u32[]{:S(2)}) collective-permute-start(bf16[2,512,1,128]{3,1,0,2:T(8,128)(2,1)S(1)} %collective-permute-done), channel_id=1, source_target_pairs={{0,4},{4,8},{8,12},{12,16},{16,20},{20,24},{24,28},{28,32},{32,36}... | collective-permute-start | bytes 786440 | tf_op jit(solution)/shard_map/ppermute | solution.py:20
  52.4 5.8 %collective-permute-done.1 = bf16[2,512,1,128]{3,1,0,2:T(8,128)(2,1)S(1)} collective-permute-done((bf16[2,512,1,128]{3,1,0,2:T(8,128)(2,1)S(1)}, bf16[2,512,1,128]{3,1,0,2:T(8,128)(2,1)S(1)}, u32[]{:S(2)}, u32[]{:S(2)}) %collective-permute-start.1) | collective-permute-done | bytes 262176 | tf_op jit(solution)/shard_map/ppermute | solution.py:20
  58.1 11.9 %collective-permute-start.2 = (bf16[2,512,1,128]{3,1,0,2:T(8,128)(2,1)S(1)}, bf16[2,512,1,128]{3,1,0,2:T(8,128)(2,1)S(1)}, u32[]{:S(2)}, u32[]{:S(2)}) collective-permute-start(bf16[2,512,1,128]{3,1,0,2:T(8,128)(2,1)S(1)} %collective-permute-done.1), channel_id=1, source_target_pairs={{0,4},{4,8},{8,12},{12,16},{16,20},{20,24},{24,28},{28,32},{32,36}... | collective-permute-start | bytes 786440 | tf_op jit(solution)/shard_map/ppermute | solution.py:20
  71.4 4.8 %collective-permute-done.2 = bf16[2,512,1,128]{3,1,0,2:T(8,128)(2,1)S(1)} collective-permute-done((bf16[2,512,1,128]{3,1,0,2:T(8,128)(2,1)S(1)}, bf16[2,512,1,128]{3,1,0,2:T(8,128)(2,1)S(1)}, u32[]{:S(2)}, u32[]{:S(2)}) %collective-permute-start.2) | collective-permute-done | bytes 262176 | tf_op jit(solution)/shard_map/ppermute | solution.py:20
  76.3 12.6 %collective-permute-start.3 = (bf16[2,512,1,128]{3,1,0,2:T(8,128)(2,1)S(1)}, bf16[2,512,1,128]{3,1,0,2:T(8,128)(2,1)S(1)}, u32[]{:S(2)}, u32[]{:S(2)}) collective-permute-start(bf16[2,512,1,128]{3,1,0,2:T(8,128)(2,1)S(1)} %collective-permute-done.2), channel_id=1, source_target_pairs={{0,4},{4,8},{8,12},{12,16},{16,20},{20,24},{24,28},{28,32},{32,36}... | collective-permute-start | bytes 786440 | tf_op jit(solution)/shard_map/ppermute | solution.py:20
  90.4 2.9 %collective-permute-done.3 = bf16[2,512,1,128]{3,1,0,2:T(8,128)(2,1)S(1)} collective-permute-done((bf16[2,512,1,128]{3,1,0,2:T(8,128)(2,1)S(1)}, bf16[2,512,1,128]{3,1,0,2:T(8,128)(2,1)S(1)}, u32[]{:S(2)}, u32[]{:S(2)}) %collective-permute-start.3) | collective-permute-done | bytes 262176 | tf_op jit(solution)/shard_map/ppermute | solution.py:20
  95.6 91.5 %while.12 = (s32[]{:T(128)}, f32[2,4,512,128]{3,2,1,0:T(8,128)}, f32[2,4,512]{2,1,0:T(4,128)}, pred[5]{0:T(512)(128)(4,1)S(1)}, s32[2]{0:T(128)S(1)}, /*index=5*...) while((s32[]{:T(128)}, f32[2,4,512,128]{3,2,1,0:T(8,128)}, ...), condition=%wide.region_26.27_spmd, body=%wide.region_5.26_spmd.sunk | while | flops 2754895872 | bytes 90399928 | solution.py:98
  99.4 2.0 %slice_bitcast_fusion.9 = (bf16[512,128]{1,0:T(8,128)(2,1)}, bf16[512,128]{1,0:T(8,128)(2,1)}, bf16[512,128]{1,0:T(8,128)(2,1)}, bf16[512,128]{1,0:T(8,128)(2,1)...) fusion(bf16[5,2,512,128]{3,2,1,0:T(8,128)(2,1)} %bitcast.162), kind=kLoop, calls=%fused_computation.89.clone.1 | loop fusion | bytes 1572864 | tf_op jit(solution)/shard_map/while/body/eval_jaxpr/squeeze | solution.py:70
  103.0 6.3 %conditional.10 = (f32[4,512,128]{2,1,0:T(8,128)S(1)}, f32[4,512]{1,0:T(4,128)}, f32[4,512]{1,0:T(4,128)S(1)}) conditional(s32[]{:T(128)} %bitcast.159, () %tuple.107, (pred[1,512,512]{1,2,0:T(8,128)(4,1)S(1)}, bf16[4,512,128]{2,1,0:T(8,128)(2,1)S(1)}, bf16[512,128]{1,0:T(8,128)(2,1)S(1)}, bf16[512,128]{1,0:T(8,128)(2,1)S(1)}) %tuple.135), branch_computations={%region_6.6_spmd, %region_7.9_spmd} | conditional | flops 550772736 | bytes 15294488 | solution.py:95
  106.9 2.3 %fusion.6 = f32[4,512,128]{2,1,0:T(8,128)S(1)} fusion(f32[4,512,512]{1,2,0:T(8,128)S(1)} %get-tuple-element.257, f32[4,512]{1,0:T(4,128)} %get-tuple-element.389, pred[512,512]{0,1:T(8,128)(4,1)S(1)} %bitcast.177, f32[4,512]{1,0:T(4,128)S(1)} %get-tuple-element.244, bf16[512,128]{1,0:T(8,128)(2,1)S(1)} %get-tuple-element.146), kind=kOutput, calls=%fused_computation.7 | convolution fusion | flops 273940480 | bytes 5652480 | tf_op jit(solution)/shard_map/while/body/eval_jaxpr/cond/branch_1_fun/gqk,kd->gqd/dot_general | solution.py:86
  109.9 6.6 %conditional.11 = ((f32[4,512,128]{2,1,0:T(8,128)S(1)}, f32[4,512]{1,0:T(4,128)}, f32[4,512]{1,0:T(4,128)S(1)})) conditional(s32[]{:T(128)} %bitcast.158, (f32[4,512,128]{2,1,0:T(8,128)S(1)}, f32[4,512]{1,0:T(4,128)}, f32[4,512]{1,0:T(4,128)S(1)}) %conditional.10, (pred[1,512,512]{1,2,0:T(8,128)(4,1)S(1)}, bf16[4,512,128]{2,1,0:T(8,128)(2,1)S(1)}, ...), branch_computations={%region_10.10_spmd, %region_11.13_spmd} | conditional | flops 551030784 | bytes 16908348 | solution.py:95
  117.1 6.6 %conditional.12 = ((f32[4,512,128]{2,1,0:T(8,128)S(1)}, f32[4,512]{1,0:T(4,128)}, f32[4,512]{1,0:T(4,128)S(1)})) conditional(s32[]{:T(128)} %bitcast.157, (f32[4,512,128]{2,1,0:T(8,128)S(1)}, f32[4,512]{1,0:T(4,128)}, f32[4,512]{1,0:T(4,128)S(1)}) %get-tuple-element.454, (pred[1,512,512]{1,2,0:T(8,128)(4,1)S(1)}, ...), branch_computations={%region_14.14_spmd, %region_15.17_spmd} | conditional | flops 551030784 | bytes 16908348 | solution.py:95
  124.2 7.7 %conditional.13 = ((f32[4,512,128]{2,1,0:T(8,128)S(1)}, f32[4,512]{1,0:T(4,128)}, f32[4,512]{1,0:T(4,128)S(1)})) conditional(s32[]{:T(128)} %bitcast.156, (f32[4,512,128]{2,1,0:T(8,128)S(1)}, f32[4,512]{1,0:T(4,128)}, f32[4,512]{1,0:T(4,128)S(1)}) %get-tuple-element.455, (pred[5,512,512]{1,2,0:T(8,128)(4,1)S(1)}, ...), branch_computations={%region_18.18_spmd, %region_19.21_spmd} | conditional | flops 551030784 | bytes 16908320 | solution.py:95
  128.5 2.8 %fusion.52 = f32[4,512,128]{2,1,0:T(8,128)S(1)} fusion(f32[4,512,512]{1,2,0:T(8,128)S(1)} %get-tuple-element.263, f32[4,512]{1,0:T(4,128)S(1)} %max.10, pred[512,512]{0,1:T(8,128)(4,1)S(1)} %slice_bitcast_fusion, f32[4,512,128]{2,1,0:T(8,128)S(1)} %get-tuple-element.161, f32[4,512]{1,0:T(4,128)S(1)} %get-tuple-element.251, ...), kind=kOutput, calls=%fused_computation.56 | convolution fusion | flops 274202624 | bytes 6701056 | tf_op jit(solution)/shard_map/while/body/eval_jaxpr/cond/branch_1_fun/gqk,kd->gqd/dot_general | solution.py:86
  132.6 7.1 %conditional.14 = (f32[1,4,512,128]{3,2,1,0:T(8,128)S(1)}, f32[1,4,512]{2,1,0:T(4,128)S(1)}) conditional(s32[]{:T(128)} %bitcast.155, (f32[4,512,128]{2,1,0:T(8,128)S(1)}, f32[4,512]{1,0:T(4,128)S(1)}) %tuple.127, (pred[5,512,512]{1,2,0:T(8,128)(4,1)S(1)}, bf16[5,2,512,128]{3,2,1,0:T(8,128)(2,1)}, bf16[4,512,128]{2,1,0:T(8,128)(2,1)S(1)}, ...), branch_computations={%region_22.22_spmd, %region_23.25_spmd} | conditional | flops 551030784 | bytes 16891920 | solution.py:95
  136.9 2.8 %fusion.72 = f32[1,4,512,128]{3,2,1,0:T(8,128)S(1)} fusion(f32[4,512,512]{1,2,0:T(8,128)S(1)} %get-tuple-element.265, f32[4,512]{1,0:T(4,128)S(1)} %max.11, pred[512,512]{0,1:T(8,128)(4,1)S(1)} %slice_bitcast_fusion.1, f32[4,512,128]{2,1,0:T(8,128)S(1)} %get-tuple-element.167, f32[4,512]{1,0:T(4,128)S(1)} %get-tuple-element.253, ...), kind=kOutput, calls=%fused_computation.76 | convolution fusion | flops 274202624 | bytes 6701056 | tf_op jit(solution)/shard_map/while/body/eval_jaxpr/cond/branch_1_fun/gqk,kd->gqd/dot_general | solution.py:86
  145.1 2.0 %slice_bitcast_fusion.9 = (bf16[512,128]{1,0:T(8,128)(2,1)}, bf16[512,128]{1,0:T(8,128)(2,1)}, bf16[512,128]{1,0:T(8,128)(2,1)}, bf16[512,128]{1,0:T(8,128)(2,1)...) fusion(bf16[5,2,512,128]{3,2,1,0:T(8,128)(2,1)} %bitcast.162), kind=kLoop, calls=%fused_computation.89.clone.1 | loop fusion | bytes 1572864 | tf_op jit(solution)/shard_map/while/body/eval_jaxpr/squeeze | solution.py:70
  148.7 6.3 %conditional.10 = (f32[4,512,128]{2,1,0:T(8,128)S(1)}, f32[4,512]{1,0:T(4,128)}, f32[4,512]{1,0:T(4,128)S(1)}) conditional(s32[]{:T(128)} %bitcast.159, () %tuple.107, (pred[1,512,512]{1,2,0:T(8,128)(4,1)S(1)}, bf16[4,512,128]{2,1,0:T(8,128)(2,1)S(1)}, bf16[512,128]{1,0:T(8,128)(2,1)S(1)}, bf16[512,128]{1,0:T(8,128)(2,1)S(1)}) %tuple.135), branch_computations={%region_6.6_spmd, %region_7.9_spmd} | conditional | flops 550772736 | bytes 15294488 | solution.py:95
  152.6 2.3 %fusion.6 = f32[4,512,128]{2,1,0:T(8,128)S(1)} fusion(f32[4,512,512]{1,2,0:T(8,128)S(1)} %get-tuple-element.257, f32[4,512]{1,0:T(4,128)} %get-tuple-element.389, pred[512,512]{0,1:T(8,128)(4,1)S(1)} %bitcast.177, f32[4,512]{1,0:T(4,128)S(1)} %get-tuple-element.244, bf16[512,128]{1,0:T(8,128)(2,1)S(1)} %get-tuple-element.146), kind=kOutput, calls=%fused_computation.7 | convolution fusion | flops 273940480 | bytes 5652480 | tf_op jit(solution)/shard_map/while/body/eval_jaxpr/cond/branch_1_fun/gqk,kd->gqd/dot_general | solution.py:86
  155.6 6.6 %conditional.11 = ((f32[4,512,128]{2,1,0:T(8,128)S(1)}, f32[4,512]{1,0:T(4,128)}, f32[4,512]{1,0:T(4,128)S(1)})) conditional(s32[]{:T(128)} %bitcast.158, (f32[4,512,128]{2,1,0:T(8,128)S(1)}, f32[4,512]{1,0:T(4,128)}, f32[4,512]{1,0:T(4,128)S(1)}) %conditional.10, (pred[1,512,512]{1,2,0:T(8,128)(4,1)S(1)}, bf16[4,512,128]{2,1,0:T(8,128)(2,1)S(1)}, ...), branch_computations={%region_10.10_spmd, %region_11.13_spmd} | conditional | flops 551030784 | bytes 16908348 | solution.py:95
  162.8 6.6 %conditional.12 = ((f32[4,512,128]{2,1,0:T(8,128)S(1)}, f32[4,512]{1,0:T(4,128)}, f32[4,512]{1,0:T(4,128)S(1)})) conditional(s32[]{:T(128)} %bitcast.157, (f32[4,512,128]{2,1,0:T(8,128)S(1)}, f32[4,512]{1,0:T(4,128)}, f32[4,512]{1,0:T(4,128)S(1)}) %get-tuple-element.454, (pred[1,512,512]{1,2,0:T(8,128)(4,1)S(1)}, ...), branch_computations={%region_14.14_spmd, %region_15.17_spmd} | conditional | flops 551030784 | bytes 16908348 | solution.py:95
  162.8 1.8 fusion.31
  170.0 7.7 %conditional.13 = ((f32[4,512,128]{2,1,0:T(8,128)S(1)}, f32[4,512]{1,0:T(4,128)}, f32[4,512]{1,0:T(4,128)S(1)})) conditional(s32[]{:T(128)} %bitcast.156, (f32[4,512,128]{2,1,0:T(8,128)S(1)}, f32[4,512]{1,0:T(4,128)}, f32[4,512]{1,0:T(4,128)S(1)}) %get-tuple-element.455, (pred[5,512,512]{1,2,0:T(8,128)(4,1)S(1)}, ...), branch_computations={%region_18.18_spmd, %region_19.21_spmd} | conditional | flops 551030784 | bytes 16908320 | solution.py:95
  174.2 2.8 %fusion.52 = f32[4,512,128]{2,1,0:T(8,128)S(1)} fusion(f32[4,512,512]{1,2,0:T(8,128)S(1)} %get-tuple-element.263, f32[4,512]{1,0:T(4,128)S(1)} %max.10, pred[512,512]{0,1:T(8,128)(4,1)S(1)} %slice_bitcast_fusion, f32[4,512,128]{2,1,0:T(8,128)S(1)} %get-tuple-element.161, f32[4,512]{1,0:T(4,128)S(1)} %get-tuple-element.251, ...), kind=kOutput, calls=%fused_computation.56 | convolution fusion | flops 274202624 | bytes 6701056 | tf_op jit(solution)/shard_map/while/body/eval_jaxpr/cond/branch_1_fun/gqk,kd->gqd/dot_general | solution.py:86
  178.3 7.1 %conditional.14 = (f32[1,4,512,128]{3,2,1,0:T(8,128)S(1)}, f32[1,4,512]{2,1,0:T(4,128)S(1)}) conditional(s32[]{:T(128)} %bitcast.155, (f32[4,512,128]{2,1,0:T(8,128)S(1)}, f32[4,512]{1,0:T(4,128)S(1)}) %tuple.127, (pred[5,512,512]{1,2,0:T(8,128)(4,1)S(1)}, bf16[5,2,512,128]{3,2,1,0:T(8,128)(2,1)}, bf16[4,512,128]{2,1,0:T(8,128)(2,1)S(1)}, ...), branch_computations={%region_22.22_spmd, %region_23.25_spmd} | conditional | flops 551030784 | bytes 16891920 | solution.py:95
  182.6 2.8 %fusion.72 = f32[1,4,512,128]{3,2,1,0:T(8,128)S(1)} fusion(f32[4,512,512]{1,2,0:T(8,128)S(1)} %get-tuple-element.265, f32[4,512]{1,0:T(4,128)S(1)} %max.11, pred[512,512]{0,1:T(8,128)(4,1)S(1)} %slice_bitcast_fusion.1, f32[4,512,128]{2,1,0:T(8,128)S(1)} %get-tuple-element.167, f32[4,512]{1,0:T(4,128)S(1)} %get-tuple-element.253, ...), kind=kOutput, calls=%fused_computation.76 | convolution fusion | flops 274202624 | bytes 6701056 | tf_op jit(solution)/shard_map/while/body/eval_jaxpr/cond/branch_1_fun/gqk,kd->gqd/dot_general | solution.py:86
  188.0 3.0 %fusion.83 = bf16[8,512,128]{2,0,1:T(8,128)(2,1)S(1)} fusion(f32[8,512,128]{2,1,0:T(8,128)} %bitcast.183, f32[8,512]{0,1:T(8,128)S(1)} %copy.96), kind=kLoop, calls=%fused_computation.101 | loop fusion | flops 1048576 | bytes 3162112 | tf_op jit(solution)/shard_map/convert_element_type | solution.py:145
  (120 shorter events, 80.2 us)
Async XLA Ops:
  0.0 0.9 copy-start
  1.6 8.3 %all-to-all-start.1 = ((bf16[128,4,128]{2,0,1:T(8,128)(2,1)}), bf16[128,4,128]{2,0,1:T(8,128)(2,1)S(1)}, u32[]{:S(2)}, u32[]{:S(2)}) async-start(bf16[128,4,128]{2,0,1:T(8,128)(2,1)} %copy_bitcast_fusion.3), calls=%async_computation.1 | async-start | bytes 262144 | tf_op jit(solution)/shard_map/all_to_all | solution.py:116
  9.9 7.9 %all-to-all-start.2 = ((bf16[128,4,128]{2,0,1:T(8,128)(2,1)}), bf16[128,4,128]{2,0,1:T(8,128)(2,1)S(1)}, u32[]{:S(2)}, u32[]{:S(2)}) async-start(bf16[128,4,128]{2,0,1:T(8,128)(2,1)} %copy_bitcast_fusion.2), calls=%async_computation.2 | async-start | bytes 262144 | tf_op jit(solution)/shard_map/all_to_all | solution.py:123
  17.8 76.2 %all-to-all-start = ((bf16[128,32,128]{2,0,1:T(8,128)(2,1)}), bf16[128,32,128]{2,0,1:T(8,128)(2,1)S(1)}, u32[]{:S(2)}, u32[]{:S(2)}) async-start(bf16[128,32,128]{2,0,1:T(8,128)(2,1)} %copy.86), calls=%async_computation | async-start | bytes 2097152 | tf_op jit(solution)/shard_map/all_to_all | solution.py:109
  21.4 15.3 %collective-permute-start = (bf16[2,512,1,128]{3,1,0,2:T(8,128)(2,1)S(1)}, bf16[2,512,1,128]{3,1,0,2:T(8,128)(2,1)S(1)}, u32[]{:S(2)}, u32[]{:S(2)}) collective-permute-start(bf16[2,512,1,128]{3,1,0,2:T(8,128)(2,1)S(1)} %pad_maximum_fusion), channel_id=1, source_target_pairs={{0,4},{4,8},{8,12},{12,16},{16,20},{20,24},{24,28},{28,32},{32,36}... | collective-permute-start | bytes 786440 | tf_op jit(solution)/shard_map/ppermute | solution.py:20
  36.7 21.4 %collective-permute-start.1 = (bf16[2,512,1,128]{3,1,0,2:T(8,128)(2,1)S(1)}, bf16[2,512,1,128]{3,1,0,2:T(8,128)(2,1)S(1)}, u32[]{:S(2)}, u32[]{:S(2)}) collective-permute-start(bf16[2,512,1,128]{3,1,0,2:T(8,128)(2,1)S(1)} %collective-permute-done), channel_id=1, source_target_pairs={{0,4},{4,8},{8,12},{12,16},{16,20},{20,24},{24,28},{28,32},{32,36}... | collective-permute-start | bytes 786440 | tf_op jit(solution)/shard_map/ppermute | solution.py:20
  58.1 18.2 %collective-permute-start.2 = (bf16[2,512,1,128]{3,1,0,2:T(8,128)(2,1)S(1)}, bf16[2,512,1,128]{3,1,0,2:T(8,128)(2,1)S(1)}, u32[]{:S(2)}, u32[]{:S(2)}) collective-permute-start(bf16[2,512,1,128]{3,1,0,2:T(8,128)(2,1)S(1)} %collective-permute-done.1), channel_id=1, source_target_pairs={{0,4},{4,8},{8,12},{12,16},{16,20},{20,24},{24,28},{28,32},{32,36}... | collective-permute-start | bytes 786440 | tf_op jit(solution)/shard_map/ppermute | solution.py:20
  76.3 17.0 %collective-permute-start.3 = (bf16[2,512,1,128]{3,1,0,2:T(8,128)(2,1)S(1)}, bf16[2,512,1,128]{3,1,0,2:T(8,128)(2,1)S(1)}, u32[]{:S(2)}, u32[]{:S(2)}) collective-permute-start(bf16[2,512,1,128]{3,1,0,2:T(8,128)(2,1)S(1)} %collective-permute-done.2), channel_id=1, source_target_pairs={{0,4},{4,8},{8,12},{12,16},{16,20},{20,24},{24,28},{28,32},{32,36}... | collective-permute-start | bytes 786440 | tf_op jit(solution)/shard_map/ppermute | solution.py:20
  109.9 4.3 %copy-start.2 = (bf16[512,128]{1,0:T(8,128)(2,1)S(1)}, bf16[512,128]{1,0:T(8,128)(2,1)}, u32[]{:S(2)}) copy-start(bf16[512,128]{1,0:T(8,128)(2,1)} %get-tuple-element.152) | copy-start | bytes 393220 | tf_op jit(solution)/shard_map/while/body/eval_jaxpr/cond
  117.1 4.3 %copy-start.1 = (bf16[512,128]{1,0:T(8,128)(2,1)S(1)}, bf16[512,128]{1,0:T(8,128)(2,1)}, u32[]{:S(2)}) copy-start(bf16[512,128]{1,0:T(8,128)(2,1)} %get-tuple-element.159) | copy-start | bytes 393220 | tf_op jit(solution)/shard_map/while/body/eval_jaxpr/cond
  132.6 8.2 %copy-start.3 = (f32[2,4,512]{2,1,0:T(4,128)S(1)}, f32[2,4,512]{2,1,0:T(4,128)}, u32[]{:S(2)}) copy-start(f32[2,4,512]{2,1,0:T(4,128)} %get-tuple-element.426) | copy-start | bytes 49156 | tf_op jit(solution)/shard_map/while
  140.8 0.6 copy-start.4
  155.6 4.3 %copy-start.2 = (bf16[512,128]{1,0:T(8,128)(2,1)S(1)}, bf16[512,128]{1,0:T(8,128)(2,1)}, u32[]{:S(2)}) copy-start(bf16[512,128]{1,0:T(8,128)(2,1)} %get-tuple-element.152) | copy-start | bytes 393220 | tf_op jit(solution)/shard_map/while/body/eval_jaxpr/cond
  162.8 4.3 %copy-start.1 = (bf16[512,128]{1,0:T(8,128)(2,1)S(1)}, bf16[512,128]{1,0:T(8,128)(2,1)}, u32[]{:S(2)}) copy-start(bf16[512,128]{1,0:T(8,128)(2,1)} %get-tuple-element.159) | copy-start | bytes 393220 | tf_op jit(solution)/shard_map/while/body/eval_jaxpr/cond
  178.3 8.2 %copy-start.3 = (f32[2,4,512]{2,1,0:T(4,128)S(1)}, f32[2,4,512]{2,1,0:T(4,128)}, u32[]{:S(2)}) copy-start(f32[2,4,512]{2,1,0:T(4,128)} %get-tuple-element.426) | copy-start | bytes 49156 | tf_op jit(solution)/shard_map/while
  186.5 0.6 copy-start.4
where the time goes:
time: 194 us; the launch traced here: 192 us
  starting transfers between devices  54.4 us (28%)
  matrix products  38.6 us (20%)
  other arithmetic  36.1 us (19%)
  local copies, waits for them, and re-layouts  29.7 us (15%)
  waiting for transfers between devices  22.9 us (12%)
  loops' own time  10.4 us (5%)
    ppermute x4, starting transfers between devices, shifted(): return lax.ppermute(block, axis, route)  43.9 us
    dot_general x10, matrix products, update(): jnp.einsum('gqk,kd->gqd', weights.astype(jnp.bfloat16), value_block, pref...  22.5 us
    ppermute x4, waiting for transfers between devices, shifted(): return lax.ppermute(block, axis, route)  22.4 us
    dot_general x10, matrix products, update(): jnp.einsum('gqd,kd->gqk', query_group, key_block, preferred_element_type=...  16.1 us
    reduce_sum x10, other arithmetic, update(): totals = totals * factor + jnp.sum(weights, axis=2)  11.8 us
    another operation x1, loops' own time, attend(): lax.map(one_group, jnp.arange(group_count, dtype=jnp.int32))  9.98 us
    unnamed x7, local copies, waits for them, and re-layouts  5.95 us
    add x8, other arithmetic, update(): totals = totals * factor + jnp.sum(weights, axis=2)  5.7 us
  transfers between devices with their start and end apart: 7, of which 6 were waited for; matrix products, arithmetic and copies ran while one was open for 8% of the time, Pallas kernels for 0%

commit v1 on v0

v1 whole, which is shorter than its diff:
```python
import functools
import math

import jax
import jax.numpy as jnp
from jax import lax
from jax.experimental import pallas as pl
from jax.experimental.pallas import tpu as pltpu
from jax.sharding import PartitionSpec as P

QUERY_HEADS = 32
KEY_VALUE_HEADS = 4
HEAD_SIZE = 128
SPAN = 4
BLOCK = 512
CHUNK = 128
BACK = SPAN * BLOCK
WINDOW = BACK + BLOCK
PACKED = 65536
HEADS = QUERY_HEADS // KEY_VALUE_HEADS
SCALE = math.log2(math.e) / math.sqrt(HEAD_SIZE)
APART = -32768.0

MESH = pl.DeviceIdType.MESH
F32 = jnp.float32
BF16 = jnp.bfloat16

STACK = 4
QROWS = 128
BAND = BACK + QROWS
TILES = [(s, min(512, BAND - s)) for s in range(0, BAND, 512)]


def nt(a, b):
    return lax.dot_general(a, b, (((1,), (1,)), ((), ())), preferred_element_type=F32)


def nn(a, b):
    return lax.dot_general(a, b, (((1,), (0,)), ((), ())), preferred_element_type=F32)


def partners(head):
    return [head, head + 1 - 2 * (head % 2), (head + 2) % 4, 3 - head]


def mark_documents(group, len_ref, kf, qf):
    lens = jnp.broadcast_to(len_ref[...], (16, 256))
    upto = (
        lax.broadcasted_iota(jnp.int32, (256, 256), 0)
        <= lax.broadcasted_iota(jnp.int32, (256, 256), 1)
    ).astype(F32).astype(BF16)
    high = (lens // 16).astype(F32).astype(BF16)
    low = (lens % 16).astype(F32).astype(BF16)
    ends = (nn(high, upto) * 16.0 + nn(low, upto))[0:1, :].astype(jnp.int32)
    ones = jnp.ones((256, 128), BF16)
    lane = lax.broadcasted_iota(jnp.int32, (512, 128), 1)
    for d in range(SPAN + 1):
        base = d * BLOCK
        pos = lax.broadcasted_iota(jnp.int32, (512, 256), 0) + (group * BLOCK + base + (PACKED - BACK)) % PACKED
        passed = jnp.where(ends <= pos, 1.0, 0.0).astype(BF16)
        index = nn(passed, ones).astype(jnp.int32)
        bit = jnp.right_shift(index, lane // 2) & 1
        differs = jnp.where(lane % 2 == 0, 1 - bit, bit)
        inside = lane < 16
        kf[base : base + BLOCK, :] = jnp.where(inside, differs.astype(F32) * APART, 0.0).astype(BF16)
        if d == SPAN:
            qf[...] = jnp.where(inside, (1 - differs).astype(F32), 0.0).astype(BF16)


def scores_into(item_heads, qt, buf, qbuf, kv, kf, qf):
    rows = slice(qt * QROWS, (qt + 1) * QROWS)
    marks = qf[rows, :]
    q = jnp.concatenate(
        [jnp.concatenate([qbuf[h, rows, :], marks], axis=1) for h in item_heads], axis=0
    )
    causal = lax.broadcasted_iota(jnp.int32, (QROWS, QROWS), 1) <= lax.broadcasted_iota(
        jnp.int32, (QROWS, QROWS), 0
    )
    causal = jnp.concatenate([causal] * STACK, axis=0)
    top = None
    for s, n in TILES:
        lo = qt * QROWS + s
        k = jnp.concatenate([kv[0, lo : lo + n, :], kf[lo : lo + n, :]], axis=1)
        sc = nt(q, k)
        if s + n == BAND:
            last = jnp.where(causal, sc[:, n - QROWS :], -1e30)
            sc = jnp.concatenate([sc[:, : n - QROWS], last], axis=1) if n > QROWS else last
        buf[:, s : s + n] = sc
        for a in range(0, n, 128):
            part = sc[:, a : a + 128]
            top = part if top is None else jnp.maximum(top, part)
    return jnp.max(top, axis=1, keepdims=True) * SCALE


def weigh(qt, buf, top, kv):
    acc = None
    for s, n in TILES:
        lo = qt * QROWS + s
        p = jnp.exp2(buf[:, s : s + n] * SCALE - top).astype(BF16)
        v = jnp.concatenate([kv[1, lo : lo + n, :], jnp.ones((n, 128), BF16)], axis=1)
        part = nn(p, v)
        acc = part if acc is None else acc + part
    return (acc[:, :128] / acc[:, 128:]).astype(BF16)


def kernel(
    len_ref, q_ref, k_ref, v_ref, o_ref,
    qbuf, kv, kf, qf, out, s0, s1,
    kv_send, kv_recv, q_send, q_recv, c_send, c_recv, o_sem,
):
    group = lax.axis_index("ctx")
    head = lax.axis_index("head")
    x = group % 4
    row = group // 4
    below = (group + 4) % 128
    above = (group + 124) % 128
    mates = partners(head)
    across = [row * 4 + (x + d) % 4 for d in range(4)]

    barrier = pltpu.get_barrier_semaphore()
    greet = [(group, m) for m in mates[1:]]
    greet += [(c, head) for c in across[1:]] + [(below, head), (above, head)]
    for who in greet:
        pl.semaphore_signal(barrier, inc=1, device_id=who, device_id_type=MESH)
    pl.semaphore_wait(barrier, len(greet))

    own = pl.ds(pl.multiple_of(head * CHUNK, CHUNK), CHUNK)
    own_kv = pl.ds(pl.multiple_of(BACK + head * CHUNK, CHUNK), CHUNK)

    def columns(start):
        return pl.ds(pl.multiple_of(start, 128), 128)

    def kv_copy(which, i):
        src = (k_ref, v_ref)[which].at[:, columns(mates[i] * 128)]
        dst = kv.at[which, own_kv, :]
        if i == 0:
            return pltpu.make_async_copy(src, dst, kv_recv.at[which, 0])
        return pltpu.make_async_remote_copy(
            src_ref=src, dst_ref=dst, send_sem=kv_send.at[which, i], recv_sem=kv_recv.at[which, i],
            device_id=(group, mates[i]), device_id_type=MESH,
        )

    def q_copy(j, i):
        src = q_ref.at[:, columns((mates[i] * HEADS + j) * 128)]
        dst = qbuf.at[j, own, :]
        if i == 0:
            return pltpu.make_async_copy(src, dst, q_recv.at[j, 0])
        return pltpu.make_async_remote_copy(
            src_ref=src, dst_ref=dst, send_sem=q_send.at[j, i], recv_sem=q_recv.at[j, i],
            device_id=(group, mates[i]), device_id_type=MESH,
        )

    def chunk(slot, i):
        return pl.ds(pl.multiple_of(slot * BLOCK + mates[i] * CHUNK, CHUNK), CHUNK)

    def ctx_copy(d, i, source):
        return pltpu.make_async_remote_copy(
            src_ref=kv.at[:, chunk(source, i), :], dst_ref=kv.at[:, chunk(SPAN - d, i), :],
            send_sem=c_send.at[d - 1, i], recv_sem=c_recv.at[d - 1, i],
            device_id=(below if d == 4 else across[d], head), device_id_type=MESH,
        )

    order = (2, 3, 1, 0)
    for i in order:
        for which in range(2):
            kv_copy(which, i).start()
    for j in range(HEADS):
        for i in order:
            q_copy(j, i).start()

    mark_documents(group, len_ref, kf, qf)

    for i in range(4):
        for which in range(2):
            if i == 0:
                kv_copy(which, i).wait()
            else:
                kv_copy(which, i).wait_recv()
        ctx_copy(4, i, SPAN).start()
        for d in (1, 3, 2):
            @pl.when(x + d < 4)
            def _(d=d, i=i):
                ctx_copy(d, i, SPAN).start()
    for i in range(4):
        ctx_copy(4, i, SPAN).wait_recv()
        for d in (1, 3, 2):
            @pl.when(x + d >= 4)
            def _(d=d, i=i):
                ctx_copy(d, i, 0).start()
    for d in (1, 3, 2):
        for i in range(4):
            ctx_copy(d, i, SPAN).wait_recv()
    for j in range(HEADS):
        for i in range(4):
            if i == 0:
                q_copy(j, i).wait()
            else:
                q_copy(j, i).wait_recv()

    bufs = (s0, s1)
    tiles_q = BLOCK // QROWS
    groups = HEADS // STACK

    def item_heads(jb):
        return [jb * STACK + h for h in range(STACK)]

    def out_copy(jb, qt):
        part = (pl.ds(qt * QROWS, QROWS), pl.ds(pl.multiple_of(jb * STACK * 128, 128), STACK * 128))
        return pltpu.make_async_copy(out.at[part], o_ref.at[part], o_sem.at[jb, qt])

    first = scores_into(item_heads(0), 0, s0, qbuf, kv, kf, qf)

    def body(jb, top):
        for qt in range(tiles_q):
            next_jb = jnp.minimum(jb + (qt + 1) // tiles_q, groups - 1)
            later = scores_into(item_heads(next_jb), (qt + 1) % tiles_q, bufs[(qt + 1) % 2], qbuf, kv, kf, qf)
            result = weigh(qt, bufs[qt % 2], top, kv)
            for h in range(STACK):
                out[qt * QROWS : (qt + 1) * QROWS, columns((jb * STACK + h) * 128)] = result[
                    h * QROWS : (h + 1) * QROWS
                ]
            out_copy(jb, qt).start()
            top = later
        return top

    lax.fori_loop(0, groups, body, first)

    for i in range(1, 4):
        for which in range(2):
            kv_copy(which, i).wait_send()
        for j in range(HEADS):
            q_copy(j, i).wait_send()
    for d in range(1, SPAN + 1):
        for i in range(4):
            ctx_copy(d, i, SPAN).wait_send()
    for jb in range(groups):
        for qt in range(tiles_q):
            out_copy(jb, qt).wait()


def shards(queries, keys, values, doc_lengths):
    anywhere = pl.BlockSpec(memory_space=pl.ANY)
    return pl.pallas_call(
        kernel,
        out_shape=jax.ShapeDtypeStruct((BLOCK, HEADS * HEAD_SIZE), BF16),
        in_specs=[pl.BlockSpec(memory_space=pltpu.VMEM), anywhere, anywhere, anywhere],
        out_specs=anywhere,
        scratch_shapes=[
            pltpu.VMEM((HEADS, BLOCK, HEAD_SIZE), BF16),
            pltpu.VMEM((2, WINDOW, HEAD_SIZE), BF16),
            pltpu.VMEM((WINDOW, HEAD_SIZE), BF16),
            pltpu.VMEM((BLOCK, HEAD_SIZE), BF16),
            pltpu.VMEM((BLOCK, HEADS * HEAD_SIZE), BF16),
            pltpu.VMEM((STACK * QROWS, BAND), F32),
            pltpu.VMEM((STACK * QROWS, BAND), F32),
            pltpu.SemaphoreType.DMA((2, 4)),
            pltpu.SemaphoreType.DMA((2, 4)),
            pltpu.SemaphoreType.DMA((HEADS, 4)),
            pltpu.SemaphoreType.DMA((HEADS, 4)),
            pltpu.SemaphoreType.DMA((SPAN, 4)),
            pltpu.SemaphoreType.DMA((SPAN, 4)),
            pltpu.SemaphoreType.DMA((HEADS // STACK, BLOCK // QROWS)),
        ],
        compiler_params=pltpu.CompilerParams(
            collective_id=0, has_side_effects=True, vmem_limit_bytes=56 * 2**20
        ),
    )(doc_lengths.reshape(1, -1), queries, keys, values)


def solution(mesh):
    placed = (P(("ctx", "head"), None), P(("ctx", "head"), None), P(("ctx", "head"), None), P())
    return jax.shard_map(
        shards, mesh=mesh, in_specs=placed, out_specs=P("ctx", "head"), check_vma=False
    )
```

time: 194 us -> 54.2 us (0.28)
  the two profiles are of different devices: /device:TPU:190 before, /device:TPU:65 now
where the time goes in v1:
time: 54.2 us; the launch traced here: 54 us
  Pallas kernels  51.8 us (96%)
  local copies, waits for them, and re-layouts  2.26 us (4%)
    pallas_call x1, Pallas kernels, shards(): pl.pallas_call(kernel, out_shape=jax.ShapeDtypeStruct((BLOCK, HEADS * HEA...  51.8 us
    unnamed x1, local copies, waits for them, and re-layouts  2.26 us

profile of v1, /device:TPU:65, one launch (start us, length us, event | category | flops | bytes accessed | tf_op | source)
XLA Modules:
  0.0 54.0 jit_solution(13698701714900839491)
XLA Ops:
  0.0 51.8 %shard_map.46 = bf16[512,1024]{1,0:T(8,128)(2,1)} custom-call(s32[1,256]{1,0:T(1,128)} %bitcast.1, bf16[128,4096]{1,0:T(8,128)(2,1)} %q_ref.1, bf16[128,512]{1,0:T(8,128)(2,1)} %k_ref.1, bf16[128,512]{1,0:T(8,128)(2,1)} %v_ref.1), custom_call_target="tpu_custom_call" | custom-call | tf_op jit(solution)/shard_map/pallas_call | solution.py:243
  51.8 2.3 %copy.6 = bf16[512,1024]{1,0:T(8,128)(2,1)} copy(bf16[512,1024]{1,0:T(8,128)(2,1)} %shard_map.46) | data formatting | bytes 2097152

commit v2 on v1

--- a/solution.py
+++ b/solution.py
@@ -28,7 +28,6 @@
 STACK = 4
 QROWS = 128
 BAND = BACK + QROWS
-TILES = [(s, min(512, BAND - s)) for s in range(0, BAND, 512)]
 
 
 def nt(a, b):
@@ -67,46 +66,43 @@
             qf[...] = jnp.where(inside, (1 - differs).astype(F32), 0.0).astype(BF16)
 
 
-def scores_into(item_heads, qt, buf, qbuf, kv, kf, qf):
-    rows = slice(qt * QROWS, (qt + 1) * QROWS)
-    marks = qf[rows, :]
-    q = jnp.concatenate(
-        [jnp.concatenate([qbuf[h, rows, :], marks], axis=1) for h in item_heads], axis=0
-    )
-    causal = lax.broadcasted_iota(jnp.int32, (QROWS, QROWS), 1) <= lax.broadcasted_iota(
-        jnp.int32, (QROWS, QROWS), 0
-    )
-    causal = jnp.concatenate([causal] * STACK, axis=0)
-    top = None
-    for s, n in TILES:
-        lo = qt * QROWS + s
+def pieces(qt):
+    reach = [(qt * QROWS, BLOCK - qt * QROWS), (BLOCK, BLOCK), (3 * BLOCK, BLOCK)]
+    return reach + [(BACK, (qt + 1) * QROWS)]
+
+
+def score(q, spans, buf, kv, kf, causal):
+    at, top = 0, None
+    for lo, n in spans:
         k = jnp.concatenate([kv[0, lo : lo + n, :], kf[lo : lo + n, :]], axis=1)
         sc = nt(q, k)
-        if s + n == BAND:
+        if lo == BACK:
             last = jnp.where(causal, sc[:, n - QROWS :], -1e30)
             sc = jnp.concatenate([sc[:, : n - QROWS], last], axis=1) if n > QROWS else last
-        buf[:, s : s + n] = sc
+        buf[:, at : at + n] = sc
         for a in range(0, n, 128):
             part = sc[:, a : a + 128]
             top = part if top is None else jnp.maximum(top, part)
-    return jnp.max(top, axis=1, keepdims=True) * SCALE
-
-
-def weigh(qt, buf, top, kv):
-    acc = None
-    for s, n in TILES:
-        lo = qt * QROWS + s
-        p = jnp.exp2(buf[:, s : s + n] * SCALE - top).astype(BF16)
+        at += n
+    return jnp.broadcast_to(jnp.max(top, axis=1, keepdims=True) * SCALE, top.shape)
+
+
+def weigh(spans, buf, top, kv):
+    at, acc = 0, None
+    for lo, n in spans:
+        shift = jnp.concatenate([top] * (n // 128), axis=1)
+        p = jnp.exp2(buf[:, at : at + n] * SCALE - shift).astype(BF16)
         v = jnp.concatenate([kv[1, lo : lo + n, :], jnp.ones((n, 128), BF16)], axis=1)
         part = nn(p, v)
         acc = part if acc is None else acc + part
-    return (acc[:, :128] / acc[:, 128:]).astype(BF16)
+        at += n
+    return acc
 
 
 def kernel(
     len_ref, q_ref, k_ref, v_ref, o_ref,
-    qbuf, kv, kf, qf, out, s0, s1,
-    kv_send, kv_recv, q_send, q_recv, c_send, c_recv, o_sem,
+    qbuf, kv, kf, qf, out, s0, s1, accs, tops,
+    kv_send, kv_recv, q_send, q_recv, c_send, c_recv, raw_send, o_sem,
 ):
     group = lax.axis_index("ctx")
     head = lax.axis_index("head")
@@ -114,15 +110,49 @@
     row = group // 4
     below = (group + 4) % 128
     above = (group + 124) % 128
+    right = row * 4 + (x + 1) % 4
+    left = row * 4 + (x + 3) % 4
+    pair = group + 1 - 2 * (x % 2)
     mates = partners(head)
-    across = [row * 4 + (x + d) % 4 for d in range(4)]
+    has_above = row > 0
+    has_below = row < 31
+    crosses = jnp.logical_and(row % 8 == 7, has_below)
+    crossed = jnp.logical_and(row % 8 == 0, has_above)
+    lower = head < 2
 
     barrier = pltpu.get_barrier_semaphore()
-    greet = [(group, m) for m in mates[1:]]
-    greet += [(c, head) for c in across[1:]] + [(below, head), (above, head)]
-    for who in greet:
+
+    def greet(who):
         pl.semaphore_signal(barrier, inc=1, device_id=who, device_id_type=MESH)
-    pl.semaphore_wait(barrier, len(greet))
+
+    for m in mates[1:]:
+        greet((group, m))
+    greet((right, head))
+    greet((left, head))
+
+    @pl.when(has_below)
+    def _():
+        greet((below, head))
+
+    @pl.when(has_above)
+    def _():
+        greet((above, head))
+
+    raw_out = jnp.logical_and(crosses, jnp.logical_not(lower))
+    raw_in = jnp.logical_and(crossed, lower)
+
+    @pl.when(raw_out)
+    def _():
+        greet((below, mates[2]))
+        greet((below, mates[3]))
+
+    @pl.when(raw_in)
+    def _():
+        greet((above, mates[2]))
+        greet((above, mates[3]))
+
+    greeters = 5 + has_below.astype(jnp.int32) + has_above.astype(jnp.int32)
+    pl.semaphore_wait(barrier, greeters + 2 * jnp.logical_or(raw_out, raw_in).astype(jnp.int32))
 
     own = pl.ds(pl.multiple_of(head * CHUNK, CHUNK), CHUNK)
     own_kv = pl.ds(pl.multiple_of(BACK + head * CHUNK, CHUNK), CHUNK)
@@ -154,85 +184,210 @@
         return pl.ds(pl.multiple_of(slot * BLOCK + mates[i] * CHUNK, CHUNK), CHUNK)
 
     def ctx_copy(d, i, source):
+        target = {1: right, 2: pair, 3: left, 4: below}[d]
         return pltpu.make_async_remote_copy(
             src_ref=kv.at[:, chunk(source, i), :], dst_ref=kv.at[:, chunk(SPAN - d, i), :],
             send_sem=c_send.at[d - 1, i], recv_sem=c_recv.at[d - 1, i],
-            device_id=(below if d == 4 else across[d], head), device_id_type=MESH,
+            device_id=(target, head), device_id_type=MESH,
+        )
+
+    def raw_copy(which, i):
+        src = (k_ref, v_ref)[which].at[:, columns(mates[i] * 128)]
+        return pltpu.make_async_remote_copy(
+            src_ref=src, dst_ref=kv.at[which, own, :],
+            send_sem=raw_send.at[which, i - 2], recv_sem=c_recv.at[3, i],
+            device_id=(below, mates[i]), device_id_type=MESH,
         )
 
     order = (2, 3, 1, 0)
     for i in order:
         for which in range(2):
             kv_copy(which, i).start()
+
+    @pl.when(raw_out)
+    def _():
+        for i in (2, 3):
+            for which in range(2):
+                raw_copy(which, i).start()
+
     for j in range(HEADS):
         for i in order:
             q_copy(j, i).start()
 
+    for d in range(1, SPAN + 1):
+        @pl.when(group < d)
+        def _(d=d):
+            kv[:, (SPAN - d) * BLOCK : (SPAN - d + 1) * BLOCK, :] = jnp.zeros((2, BLOCK, HEAD_SIZE), BF16)
+
     mark_documents(group, len_ref, kf, qf)
 
-    for i in range(4):
+    def sends_below(i):
+        if i < 2:
+            return has_below
+        return jnp.logical_and(has_below, jnp.logical_not(jnp.logical_and(crosses, lower)))
+
+    def takes(d):
+        return group >= d
+
+    own_right = x < 3
+    own_left = x == 0
+    up_right = jnp.logical_and(x == 3, has_above)
+    up_left = jnp.logical_and(x > 0, has_above)
+    sends_right = jnp.logical_or(own_right, up_right)
+    sends_left = jnp.logical_or(own_left, up_left)
+    sends_pair = jnp.logical_or(x >= 2, has_above)
+    even = x % 2 == 0
+
+    def stage_own(i):
         for which in range(2):
             if i == 0:
                 kv_copy(which, i).wait()
             else:
                 kv_copy(which, i).wait_recv()
-        ctx_copy(4, i, SPAN).start()
-        for d in (1, 3, 2):
-            @pl.when(x + d < 4)
-            def _(d=d, i=i):
-                ctx_copy(d, i, SPAN).start()
+
+        @pl.when(sends_below(i))
+        def _():
+            ctx_copy(4, i, SPAN).start()
+
+        @pl.when(own_right)
+        def _():
+            ctx_copy(1, i, SPAN).start()
+
+        @pl.when(own_left)
+        def _():
+            ctx_copy(3, i, SPAN).start()
+
+    def stage_up(i):
+        @pl.when(has_above)
+        def _():
+            ctx_copy(4, i, SPAN).wait_recv()
+
+        @pl.when(up_right)
+        def _():
+            ctx_copy(1, i, 0).start()
+
+        @pl.when(up_left)
+        def _():
+            ctx_copy(3, i, 0).start()
+
+    def stage_pair(i):
+        @pl.when(takes(1))
+        def _():
+            ctx_copy(1, i, SPAN).wait_recv()
+
+        @pl.when(takes(3))
+        def _():
+            ctx_copy(3, i, SPAN).wait_recv()
+
+        @pl.when(jnp.logical_and(sends_pair, even))
+        def _():
+            ctx_copy(2, i, SPAN - 1).start()
+
+        @pl.when(jnp.logical_and(sends_pair, jnp.logical_not(even)))
+        def _():
+            ctx_copy(2, i, SPAN - 3).start()
+
     for i in range(4):
-        ctx_copy(4, i, SPAN).wait_recv()
-        for d in (1, 3, 2):
-            @pl.when(x + d >= 4)
-            def _(d=d, i=i):
-                ctx_copy(d, i, 0).start()
-    for d in (1, 3, 2):
-        for i in range(4):
-            ctx_copy(d, i, SPAN).wait_recv()
-    for j in range(HEADS):
-        for i in range(4):
-            if i == 0:
-                q_copy(j, i).wait()
-            else:
-                q_copy(j, i).wait_recv()
+        stage_own(i)
+    stage_up(0)
+    stage_up(1)
+    stage_pair(0)
+    stage_up(2)
+    stage_pair(1)
+    stage_up(3)
+    stage_pair(2)
+    stage_pair(3)
 
     bufs = (s0, s1)
     tiles_q = BLOCK // QROWS
     groups = HEADS // STACK
-
-    def item_heads(jb):
-        return [jb * STACK + h for h in range(STACK)]
+    causal = lax.broadcasted_iota(jnp.int32, (QROWS, QROWS), 1) <= lax.broadcasted_iota(
+        jnp.int32, (QROWS, QROWS), 0
+    )
+    causal = jnp.concatenate([causal] * STACK, axis=0)
+    two_back = [(2 * BLOCK, BLOCK)]
+
+    def rows_of(jb, qt):
+        rows = slice(qt * QROWS, (qt + 1) * QROWS)
+        marks = qf[rows, :]
+        return jnp.concatenate(
+            [jnp.concatenate([qbuf[jb * STACK + h, rows, :], marks], axis=1) for h in range(STACK)], axis=0
+        )
 
     def out_copy(jb, qt):
         part = (pl.ds(qt * QROWS, QROWS), pl.ds(pl.multiple_of(jb * STACK * 128, 128), STACK * 128))
         return pltpu.make_async_copy(out.at[part], o_ref.at[part], o_sem.at[jb, qt])
 
-    first = scores_into(item_heads(0), 0, s0, qbuf, kv, kf, qf)
-
-    def body(jb, top):
+    def early(jb, _):
+        for h in range(STACK):
+            for i in range(4):
+                if i == 0:
+                    q_copy(jb * STACK + h, i).wait()
+                else:
+                    q_copy(jb * STACK + h, i).wait_recv()
+
+        def finish(qt, top):
+            accs[jb, qt] = weigh(pieces(qt), bufs[qt % 2], top, kv)
+            tops[jb, qt] = top
+
+        before = None
         for qt in range(tiles_q):
-            next_jb = jnp.minimum(jb + (qt + 1) // tiles_q, groups - 1)
-            later = scores_into(item_heads(next_jb), (qt + 1) % tiles_q, bufs[(qt + 1) % 2], qbuf, kv, kf, qf)
-            result = weigh(qt, bufs[qt % 2], top, kv)
+            top = score(rows_of(jb, qt), pieces(qt), bufs[qt % 2], kv, kf, causal)
+            if qt:
+                finish(qt - 1, before)
+            before = top
+        finish(tiles_q - 1, before)
+        return 0
+
+    lax.fori_loop(0, groups, early, 0)
+
+    for i in range(4):
+        @pl.when(takes(2))
+        def _(i=i):
+            ctx_copy(2, i, SPAN).wait_recv()
+
+    def late(jb, _):
+        def finish(qt, top):
+            earlier = tops[jb, qt]
+            both = jnp.maximum(earlier, top)
+            factor = jnp.exp2(earlier - both)
+            acc = accs[jb, qt] * jnp.concatenate([factor, factor], axis=1)
+            acc = acc + weigh(two_back, bufs[qt % 2], both, kv)
+            result = (acc[:, :128] / acc[:, 128:]).astype(BF16)
             for h in range(STACK):
                 out[qt * QROWS : (qt + 1) * QROWS, columns((jb * STACK + h) * 128)] = result[
                     h * QROWS : (h + 1) * QROWS
                 ]
             out_copy(jb, qt).start()
-            top = later
-        return top
-
-    lax.fori_loop(0, groups, body, first)
+
+        before = None
+        for qt in range(tiles_q):
+            top = score(rows_of(jb, qt), two_back, bufs[qt % 2], kv, kf, causal)
+            if qt:
+                finish(qt - 1, before)
+            before = top
+        finish(tiles_q - 1, before)
+        return 0
+
+    lax.fori_loop(0, groups, late, 0)
 
     for i in range(1, 4):
         for which in range(2):
             kv_copy(which, i).wait_send()
         for j in range(HEADS):
             q_copy(j, i).wait_send()
-    for d in range(1, SPAN + 1):
-        for i in range(4):
-            ctx_copy(d, i, SPAN).wait_send()
+
+    @pl.when(raw_out)
+    def _():
+        for i in (2, 3):
+            for which in range(2):
+                raw_copy(which, i).wait_send()
+
+    for i in range(4):
+        for d, sends in ((1, sends_right), (2, sends_pair), (3, sends_left), (4, sends_below(i))):
+            @pl.when(sends)
+            def _(d=d, i=i):
+                ctx_copy(d, i, SPAN).wait_send()
     for jb in range(groups):
         for qt in range(tiles_q):
             out_copy(jb, qt).wait()
@@ -240,6 +395,8 @@
 
 def shards(queries, keys, values, doc_lengths):
     anywhere = pl.BlockSpec(memory_space=pl.ANY)
+    stacked = STACK * QROWS
+    items = (HEADS // STACK, BLOCK // QROWS)
     return pl.pallas_call(
         kernel,
         out_shape=jax.ShapeDtypeStruct((BLOCK, HEADS * HEAD_SIZE), BF16),
@@ -251,15 +408,18 @@
             pltpu.VMEM((WINDOW, HEAD_SIZE), BF16),
             pltpu.VMEM((BLOCK, HEAD_SIZE), BF16),
             pltpu.VMEM((BLOCK, HEADS * HEAD_SIZE), BF16),
-            pltpu.VMEM((STACK * QROWS, BAND), F32),
-            pltpu.VMEM((STACK * QROWS, BAND), F32),
+            pltpu.VMEM((stacked, BAND - BLOCK), F32),
+            pltpu.VMEM((stacked, BAND - BLOCK), F32),
+            pltpu.VMEM((*items, stacked, 2 * HEAD_SIZE), F32),
+            pltpu.VMEM((*items, stacked, HEAD_SIZE), F32),
             pltpu.SemaphoreType.DMA((2, 4)),
             pltpu.SemaphoreType.DMA((2, 4)),
             pltpu.SemaphoreType.DMA((HEADS, 4)),
             pltpu.SemaphoreType.DMA((HEADS, 4)),
             pltpu.SemaphoreType.DMA((SPAN, 4)),
             pltpu.SemaphoreType.DMA((SPAN, 4)),
-            pltpu.SemaphoreType.DMA((HEADS // STACK, BLOCK // QROWS)),
+            pltpu.SemaphoreType.DMA((2, 2)),
+            pltpu.SemaphoreType.DMA(items),
         ],
         compiler_params=pltpu.CompilerParams(
             collective_id=0, has_side_effects=True, vmem_limit_bytes=56 * 2**20

time: 54.2 us -> 43 us (0.79)
  the two profiles are of different devices: /device:TPU:65 before, /device:TPU:320 now
where the time goes in v2:
time: 43 us; the launch traced here: 42.8 us
  Pallas kernels  40.5 us (94%)
  local copies, waits for them, and re-layouts  2.26 us (5%)
    pallas_call x1, Pallas kernels, shards(): pl.pallas_call(kernel, out_shape=jax.ShapeDtypeStruct((BLOCK, HEADS * HEA...  40.5 us
    unnamed x1, local copies, waits for them, and re-layouts  2.26 us

profile of v2, /device:TPU:320, one launch (start us, length us, event | category | flops | bytes accessed | tf_op | source)
XLA Modules:
  0.0 42.8 jit_solution(10674251402028593638)
XLA Ops:
  0.0 40.5 %shard_map.46 = bf16[512,1024]{1,0:T(8,128)(2,1)} custom-call(s32[1,256]{1,0:T(1,128)} %bitcast.1, bf16[128,4096]{1,0:T(8,128)(2,1)} %q_ref.1, bf16[128,512]{1,0:T(8,128)(2,1)} %k_ref.1, bf16[128,512]{1,0:T(8,128)(2,1)} %v_ref.1), custom_call_target="tpu_custom_call" | custom-call | tf_op jit(solution)/shard_map/pallas_call | solution.py:400
  40.6 2.3 %copy.6 = bf16[512,1024]{1,0:T(8,128)(2,1)} copy(bf16[512,1024]{1,0:T(8,128)(2,1)} %shard_map.46) | data formatting | bytes 2097152

commit v3 on v2

--- a/solution.py
+++ b/solution.py
@@ -66,9 +66,12 @@
             qf[...] = jnp.where(inside, (1 - differs).astype(F32), 0.0).astype(BF16)
 
 
-def pieces(qt):
-    reach = [(qt * QROWS, BLOCK - qt * QROWS), (BLOCK, BLOCK), (3 * BLOCK, BLOCK)]
-    return reach + [(BACK, (qt + 1) * QROWS)]
+def near(qt):
+    return [(BACK, (qt + 1) * QROWS), (qt * QROWS, BLOCK - qt * QROWS)]
+
+
+MIDDLE = [(3 * BLOCK, BLOCK), (BLOCK, BLOCK)]
+LAST = [(2 * BLOCK, BLOCK)]
 
 
 def score(q, spans, buf, kv, kf, causal):
@@ -287,16 +290,25 @@
         def _():
             ctx_copy(2, i, SPAN - 3).start()
 
-    for i in range(4):
-        stage_own(i)
-    stage_up(0)
+    stage_own(0)
+    stage_own(1)
+
+    @pl.when(jnp.logical_not(crossed))
+    def _():
+        stage_up(0)
+
+    stage_own(2)
+    stage_own(3)
+
+    @pl.when(crossed)
+    def _():
+        stage_up(0)
+
     stage_up(1)
+    stage_up(2)
     stage_pair(0)
-    stage_up(2)
+    stage_up(3)
     stage_pair(1)
-    stage_up(3)
-    stage_pair(2)
-    stage_pair(3)
 
     bufs = (s0, s1)
     tiles_q = BLOCK // QROWS
@@ -305,7 +317,6 @@
         jnp.int32, (QROWS, QROWS), 0
     )
     causal = jnp.concatenate([causal] * STACK, axis=0)
-    two_back = [(2 * BLOCK, BLOCK)]
 
     def rows_of(jb, qt):
         rows = slice(qt * QROWS, (qt + 1) * QROWS)
@@ -318,7 +329,7 @@
         part = (pl.ds(qt * QROWS, QROWS), pl.ds(pl.multiple_of(jb * STACK * 128, 128), STACK * 128))
         return pltpu.make_async_copy(out.at[part], o_ref.at[part], o_sem.at[jb, qt])
 
-    def early(jb, _):
+    def take_queries(jb):
         for h in range(STACK):
             for i in range(4):
                 if i == 0:
@@ -326,50 +337,88 @@
                 else:
                     q_copy(jb * STACK + h, i).wait_recv()
 
-        def finish(qt, top):
-            accs[jb, qt] = weigh(pieces(qt), bufs[qt % 2], top, kv)
-            tops[jb, qt] = top
-
-        before = None
-        for qt in range(tiles_q):
-            top = score(rows_of(jb, qt), pieces(qt), bufs[qt % 2], kv, kf, causal)
-            if qt:
-                finish(qt - 1, before)
-            before = top
-        finish(tiles_q - 1, before)
-        return 0
-
-    lax.fori_loop(0, groups, early, 0)
-
-    for i in range(4):
+    def give(jb, qt, acc):
+        result = (acc[:, :128] / acc[:, 128:]).astype(BF16)
+        for h in range(STACK):
+            out[qt * QROWS : (qt + 1) * QROWS, columns((jb * STACK + h) * 128)] = result[
+                h * QROWS : (h + 1) * QROWS
+            ]
+        out_copy(jb, qt).start()
+
+    def chain(items):
+        pending = None
+        for n, (jb, qt, spans, finish, ahead) in enumerate(items):
+            if ahead is not None:
+                ahead()
+            top = score(rows_of(jb, qt), spans, bufs[n % 2], kv, kf, causal)
+            if pending is not None:
+                pending()
+            pending = functools.partial(finish, jb, qt, spans, bufs[n % 2], top)
+        pending()
+
+    def begin(jb, qt, spans, buf, top):
+        accs[jb, qt] = weigh(spans, buf, top, kv)
+        tops[jb, qt] = top
+
+    def merged(jb, qt, spans, buf, top):
+        earlier = tops[jb, qt]
+        both = jnp.maximum(earlier, top)
+        factor = jnp.exp2(earlier - both)
+        acc = accs[jb, qt] * jnp.concatenate([factor, factor], axis=1)
+        return acc + weigh(spans, buf, both, kv), both
+
+    def go_on(jb, qt, spans, buf, top):
+        accs[jb, qt], tops[jb, qt] = merged(jb, qt, spans, buf, top)
+
+    def close(jb, qt, spans, buf, top):
+        give(jb, qt, merged(jb, qt, spans, buf, top)[0])
+
+    def alone(jb, qt, spans, buf, top):
+        give(jb, qt, weigh(spans, buf, top, kv))
+
+    def wait_middle(jb):
+        @pl.when(jb == 0)
+        def _():
+            stage_pair(2)
+            stage_pair(3)
+
+    def wait_last():
         @pl.when(takes(2))
-        def _(i=i):
-            ctx_copy(2, i, SPAN).wait_recv()
-
-    def late(jb, _):
-        def finish(qt, top):
-            earlier = tops[jb, qt]
-            both = jnp.maximum(earlier, top)
-            factor = jnp.exp2(earlier - both)
-            acc = accs[jb, qt] * jnp.concatenate([factor, factor], axis=1)
-            acc = acc + weigh(two_back, bufs[qt % 2], both, kv)
-            result = (acc[:, :128] / acc[:, 128:]).astype(BF16)
-            for h in range(STACK):
-                out[qt * QROWS : (qt + 1) * QROWS, columns((jb * STACK + h) * 128)] = result[
-                    h * QROWS : (h + 1) * QROWS
-                ]
-            out_copy(jb, qt).start()
-
-        before = None
-        for qt in range(tiles_q):
-            top = score(rows_of(jb, qt), two_back, bufs[qt % 2], kv, kf, causal)
-            if qt:
-                finish(qt - 1, before)
-            before = top
-        finish(tiles_q - 1, before)
-        return 0
-
-    lax.fori_loop(0, groups, late, 0)
+        def _():
+            for i in range(4):
+                ctx_copy(2, i, SPAN).wait_recv()
+
+    @pl.when(group > 0)
+    def _():
+        def early(jb, _):
+            take_queries(jb)
+            items = [(jb, qt, near(qt), begin, None) for qt in range(tiles_q)]
+            for qt in range(tiles_q):
+                ahead = functools.partial(wait_middle, jb) if qt == 0 else None
+                items.append((jb, qt, MIDDLE, go_on, ahead))
+            chain(items)
+            return 0
+
+        lax.fori_loop(0, groups, early, 0)
+        wait_last()
+
+        def late(jb, _):
+            chain([(jb, qt, LAST, close, None) for qt in range(tiles_q)])
+            return 0
+
+        lax.fori_loop(0, groups, late, 0)
+
+    @pl.when(group == 0)
+    def _():
+        stage_pair(2)
+        stage_pair(3)
+
+        def first(jb, _):
+            take_queries(jb)
+            chain([(jb, qt, near(qt)[:1], alone, None) for qt in range(tiles_q)])
+            return 0
+
+        lax.fori_loop(0, groups, first, 0)
 
     for i in range(1, 4):
         for which in range(2):
@@ -408,8 +457,8 @@
             pltpu.VMEM((WINDOW, HEAD_SIZE), BF16),
             pltpu.VMEM((BLOCK, HEAD_SIZE), BF16),
             pltpu.VMEM((BLOCK, HEADS * HEAD_SIZE), BF16),
-            pltpu.VMEM((stacked, BAND - BLOCK), F32),
-            pltpu.VMEM((stacked, BAND - BLOCK), F32),
+            pltpu.VMEM((stacked, 2 * BLOCK), F32),
+            pltpu.VMEM((stacked, 2 * BLOCK), F32),
             pltpu.VMEM((*items, stacked, 2 * HEAD_SIZE), F32),
             pltpu.VMEM((*items, stacked, HEAD_SIZE), F32),
             pltpu.SemaphoreType.DMA((2, 4)),

time: 43 us -> 40.8 us (0.949)
  Pallas kernels: 40.5 us -> 38.3 us
    pallas_call x1, Pallas kernels: 40.5 us -> 38.3 us  [shards(): pl.pallas_call(kernel, out_shape=jax.ShapeDtypeStruct((BLOCK, HEADS * HEA...]
where the time goes in v3:
time: 40.8 us; the launch traced here: 40.6 us
  Pallas kernels  38.3 us (94%)
  local copies, waits for them, and re-layouts  2.26 us (6%)
    pallas_call x1, Pallas kernels, shards(): pl.pallas_call(kernel, out_shape=jax.ShapeDtypeStruct((BLOCK, HEADS * HEA...  38.3 us
    unnamed x1, local copies, waits for them, and re-layouts  2.26 us

profile of v3, /device:TPU:320, one launch (start us, length us, event | category | flops | bytes accessed | tf_op | source)
XLA Modules:
  0.0 40.6 jit_solution(16485801190035979896)
XLA Ops:
  0.0 38.3 %shard_map.46 = bf16[512,1024]{1,0:T(8,128)(2,1)} custom-call(s32[1,256]{1,0:T(1,128)} %bitcast.1, bf16[128,4096]{1,0:T(8,128)(2,1)} %q_ref.1, bf16[128,512]{1,0:T(8,128)(2,1)} %k_ref.1, bf16[128,512]{1,0:T(8,128)(2,1)} %v_ref.1), custom_call_target="tpu_custom_call" | custom-call | tf_op jit(solution)/shard_map/pallas_call | solution.py:449
  38.4 2.3 %copy.6 = bf16[512,1024]{1,0:T(8,128)(2,1)} copy(bf16[512,1024]{1,0:T(8,128)(2,1)} %shard_map.46) | data formatting | bytes 2097152

commit v4 on v3

--- a/solution.py
+++ b/solution.py
@@ -213,9 +213,21 @@
             for which in range(2):
                 raw_copy(which, i).start()
 
-    for j in range(HEADS):
-        for i in order:
-            q_copy(j, i).start()
+    def send_queries(first, last, to):
+        for j in range(first, last):
+            for i in to:
+                q_copy(j, i).start()
+
+    yields = jnp.logical_and(crossed, lower)
+    send_queries(0, STACK, order)
+
+    @pl.when(jnp.logical_not(yields))
+    def _():
+        send_queries(STACK, HEADS, order)
+
+    @pl.when(yields)
+    def _():
+        send_queries(STACK, HEADS, (1, 0))
 
     for d in range(1, SPAN + 1):
         @pl.when(group < d)
@@ -308,6 +320,11 @@
     stage_up(2)
     stage_pair(0)
     stage_up(3)
+
+    @pl.when(yields)
+    def _():
+        send_queries(STACK, HEADS, (2, 3))
+
     stage_pair(1)
 
     bufs = (s0, s1)

time: 40.8 us -> 40.8 us (level)
  no operation moved by 1% of the time
where the time goes in v4:
time: 40.8 us; the launch traced here: 40.6 us
  Pallas kernels  38.3 us (94%)
  local copies, waits for them, and re-layouts  2.26 us (6%)
    pallas_call x1, Pallas kernels, shards(): pl.pallas_call(kernel, out_shape=jax.ShapeDtypeStruct((BLOCK, HEADS * HEA...  38.3 us
    unnamed x1, local copies, waits for them, and re-layouts  2.26 us

profile of v4, /device:TPU:320, one launch (start us, length us, event | category | flops | bytes accessed | tf_op | source)
XLA Modules:
  0.0 40.6 jit_solution(7734319515809536605)
XLA Ops:
  0.0 38.3 %shard_map.46 = bf16[512,1024]{1,0:T(8,128)(2,1)} custom-call(s32[1,256]{1,0:T(1,128)} %bitcast.1, bf16[128,4096]{1,0:T(8,128)(2,1)} %q_ref.1, bf16[128,512]{1,0:T(8,128)(2,1)} %k_ref.1, bf16[128,512]{1,0:T(8,128)(2,1)} %v_ref.1), custom_call_target="tpu_custom_call" | custom-call | tf_op jit(solution)/shard_map/pallas_call | solution.py:466
  38.4 2.3 %copy.6 = bf16[512,1024]{1,0:T(8,128)(2,1)} copy(bf16[512,1024]{1,0:T(8,128)(2,1)} %shard_map.46) | data formatting | bytes 2097152
